TPU v7x, 32 devices: a whole 2x2x4 slice. The times are simulated.
32 devices in a mesh: grp: 4 (over y, x), mem: 8 (over z, core).
Axes of the slice: x: 2, y: 2, z: 4, core: 2. Of those that a mesh axis runs over, the one named last changes fastest.
Arguments:
- pno: bfloat16 [1024, 512, 128], P(('grp', 'mem')), may hold values from -0.5 to 0.5
- amplitudes: bfloat16 [1024, 128, 128], P(('grp', 'mem')), may hold values from -6 to 6
- pno_count: int32 [1024], P(('grp', 'mem')), may hold values from 64 to 128
- pao_coupling: bfloat16 [512, 512], replicated, may hold values from -0.25 to 0.25
- row_owner: int32 [2048, 1], P(('grp', 'mem')), may hold values from 0 to 7; in each aligned block of 64 rows (0 to 63, 64 to 127, ...) at most 16 rows name the same one
- row_pair: int32 [2048], P(('grp', 'mem')), may hold values from 0 to 31
- row_target: int32 [2048], P(('grp', 'mem')), may hold values from 0 to 31
- row_coef: float32 [2048], P(('grp', 'mem')), may hold values from -6 to 6
- column_owner: int32 [512, 1], P(('grp', 'mem')), may hold values from 0 to 3; in each aligned block of 16 rows (0 to 15, 16 to 31, ...) at most 8 rows name the same one
- column_pair: int32 [512], P(('grp', 'mem')), may hold values from 0 to 31
- column_target: int32 [512], P(('grp', 'mem')), may hold values from 0 to 31
- column_coef: float32 [512], P(('grp', 'mem')), may hold values from -6 to 6
Outputs:
- coupling_residual: float32 [1024, 128, 128], P(('grp', 'mem'))
Inputs may be any that keep to these rules, and one draw needn't show every extreme that they name: `row_owner`: among one device's in-group couplings at most 16 name the same member index, and some device's rows reach it. `column_owner`: among one device's cross-group couplings at most 8 name the same group index, and some device's rows reach it.
All inputs are finite; a program needn't handle non-finite values.
Results may differ from a plain program's by a relative error of at most 0.0064.
Values may be sent and summed in bfloat16 or wider, within the bound.
No kernel may reach another device: no remote copies, remote signals or barrier semaphores. Data moves between devices by JAX's collectives and lax.ppermute only.
A program may use at most 128 MiB of HBM per device.

v0:
```python
import jax
import jax.numpy as jnp
from jax import lax
from jax.sharding import PartitionSpec as P


def masked_blocks(pno, amplitudes, pno_count):
    width = pno.shape[2]
    live = jnp.arange(width, dtype=jnp.int32)[None, :] < pno_count[:, None]
    live_pno = jnp.where(live[:, None, :], pno, jnp.zeros((), pno.dtype))
    live_amp = jnp.where(
        live[:, :, None] & live[:, None, :], amplitudes, jnp.zeros((), amplitudes.dtype)
    )
    return (live_pno, live_amp)


def metric_blocks(live_pno, pao_coupling):
    mixed = jnp.einsum("kj,tkp->tjp", pao_coupling, live_pno, preferred_element_type=jnp.float32)
    return (live_pno.astype(jnp.float32) + mixed).astype(jnp.bfloat16)


def coupling_terms(metric_rows, source_pno, source_amp):
    intersection = jnp.einsum(
        "tkp,tkq->tpq", metric_rows, source_pno, preferred_element_type=jnp.float32
    ).astype(jnp.bfloat16)
    half = jnp.einsum(
        "tpq,tqr->tpr", intersection, source_amp, preferred_element_type=jnp.float32
    ).astype(jnp.bfloat16)
    return jnp.einsum("tpr,tsr->tps", half, intersection, preferred_element_type=jnp.float32)


def slot_layout(owner, peers, capacity):
    onehot = (owner[:, None] == jnp.arange(peers, dtype=jnp.int32)[None, :]).astype(jnp.int32)
    before = jnp.cumsum(onehot, axis=0) - onehot
    rank = jnp.sum(before * onehot, axis=1)
    return owner * capacity + rank


def pair_total(target, terms, pairs):
    onehot = (jnp.arange(pairs, dtype=jnp.int32)[:, None] == target[None, :]).astype(jnp.float32)
    return jnp.einsum("at,tps->aps", onehot, terms, precision=lax.Precision.HIGHEST)


def shards(
    pno,
    amplitudes,
    pno_count,
    pao_coupling,
    row_owner,
    row_pair,
    row_target,
    row_coef,
    column_owner,
    column_pair,
    column_target,
    column_coef,
):
    pairs, width_k, width_p = pno.shape
    members = lax.axis_size("mem")
    groups = lax.axis_size("grp")
    row_cap = max(2, 2 * row_pair.shape[0] // members)
    col_cap = max(2, 2 * column_pair.shape[0] // groups)
    live_pno, live_amp = masked_blocks(pno, amplitudes, pno_count)
    metric = metric_blocks(live_pno, pao_coupling)
    row_metric = metric[row_target]
    col_metric = metric[column_target]
    row_slot = slot_layout(row_owner[:, 0], members, row_cap)
    wanted = jnp.zeros((members * row_cap,), jnp.int32).at[row_slot].set(row_pair)
    asked = lax.all_to_all(
        wanted.reshape(members, row_cap), "mem", split_axis=0, concat_axis=0, tiled=True
    )
    flat = asked.reshape(-1)
    sent_pno = live_pno[flat].reshape(members, row_cap, width_k, width_p)
    sent_amp = live_amp[flat].reshape(members, row_cap, width_p, width_p)
    got_pno, got_amp = (
        lax.all_to_all(sent_pno, "mem", split_axis=0, concat_axis=0, tiled=True),
        lax.all_to_all(sent_amp, "mem", split_axis=0, concat_axis=0, tiled=True),
    )
    source_pno = got_pno.reshape(members * row_cap, width_k, width_p)[row_slot]
    source_amp = got_amp.reshape(members * row_cap, width_p, width_p)[row_slot]
    row_terms = coupling_terms(row_metric, source_pno, source_amp)
    row_terms = row_coef[:, None, None] * row_terms
    col_slot = slot_layout(column_owner[:, 0], groups, col_cap)
    wanted_cols = jnp.zeros((groups * col_cap,), jnp.int32).at[col_slot].set(column_pair)
    asked_cols = lax.all_to_all(
        wanted_cols.reshape(groups, col_cap), "grp", split_axis=0, concat_axis=0, tiled=True
    )
    flat_cols = asked_cols.reshape(-1)
    out_pno = live_pno[flat_cols].reshape(groups, col_cap, width_k, width_p)
    out_amp = live_amp[flat_cols].reshape(groups, col_cap, width_p, width_p)
    back_pno, back_amp = (
        lax.all_to_all(out_pno, "grp", split_axis=0, concat_axis=0, tiled=True),
        lax.all_to_all(out_amp, "grp", split_axis=0, concat_axis=0, tiled=True),
    )
    col_pno = back_pno.reshape(groups * col_cap, width_k, width_p)[col_slot]
    col_amp = back_amp.reshape(groups * col_cap, width_p, width_p)[col_slot]
    col_terms = column_coef[:, None, None] * coupling_terms(col_metric, col_pno, col_amp)
    return -(pair_total(row_target, row_terms, pairs) + pair_total(column_target, col_terms, pairs))


def solution(mesh):
    in_specs = (
        P(("grp", "mem"), None, None),
        P(("grp", "mem"), None, None),
        P(("grp", "mem")),
        P(),
        P(("grp", "mem"), None),
        P(("grp", "mem")),
        P(("grp", "mem")),
        P(("grp", "mem")),
        P(("grp", "mem"), None),
        P(("grp", "mem")),
        P(("grp", "mem")),
        P(("grp", "mem")),
    )
    out_specs = P(("grp", "mem"), None, None)
    return jax.shard_map(shards, mesh=mesh, in_specs=in_specs, out_specs=out_specs, check_vma=False)
```

profile of v0, /device:TPU:0, one launch (start us, length us, event | category | flops | bytes accessed | tf_op | source)
XLA Modules:
  0.0 622.7 jit_solution(8336077040019060362)
XLA Ops:
  3.7 5.2 all-to-all-start.3
  15.3 4.9 all-to-all-start
  25.8 4.2 all-to-all-start.5
  30.0 6.4 %copy.19 = bf16[32,512,128]{1,2,0:T(8,128)(2,1)} copy(bf16[32,512,128]{2,1,0:T(8,128)(2,1)} %param.12) | data formatting | bytes 8388608 | tf_op args[0]
  36.4 3.9 broadcast_select_fusion
  40.3 4.9 gather_fusion.6
  46.2 4.8 all-to-all-start.4
  51.8 3.1 gather_fusion.3
  54.9 43.6 %all-to-all-done.4 = bf16[4,8,512,128]{2,3,1,0:T(8,128)(2,1)} async-done(((bf16[4,8,512,128]{2,3,1,0:T(8,128)(2,1)}), bf16[4,8,512,128]{2,3,1,0:T(8,128)(2,1)}, u32[]{:S(2)}, u32[]{:S(2)}) %all-to-all-start.4) | async-done | bytes 4194336 | tf_op jit(solution)/shard_map/all_to_all | solution.py:92
  98.5 4.6 all-to-all-start.2
  103.0 10.1 %gather_fusion.1 = bf16[128,512,128]{1,2,0:T(8,128)(2,1)} fusion(bf16[32,512,128]{1,2,0:T(8,128)(2,1)} %broadcast_select_fusion, s32[1024]{0:T(1024)S(1)} %pad_clamp_fusion.4), kind=kCustom, calls=%fused_computation.1 | custom fusion | bytes 33554944 | tf_op jit(solution)/shard_map/gather | solution.py:73
  113.1 83.9 %all-to-all-done.2 = bf16[8,16,128,128]{3,2,1,0:T(8,128)(2,1)} async-done(((bf16[8,16,128,128]{3,2,1,0:T(8,128)(2,1)}), bf16[8,16,128,128]{3,2,1,0:T(8,128)(2,1)}, u32[]{:S(2)}, u32[]{:S(2)}) %all-to-all-start.2) | async-done | bytes 4194336 | tf_op jit(solution)/shard_map/all_to_all | solution.py:77
  197.0 6.1 all-to-all-start.1
  203.2 7.8 %fusion = bf16[32,512,128]{1,2,0:T(8,128)(2,1)} fusion(bf16[32,512,128]{1,2,0:T(8,128)(2,1)} %broadcast_select_fusion, bf16[512,512]{1,0:T(8,128)(2,1)S(1)} %copy-done), kind=kOutput, calls=%fused_computation.13 | convolution fusion | flops 2153775104 | bytes 8912896 | tf_op jit(solution)/shard_map/kj,tkp->tjp/dot_general | solution.py:18
  211.0 7.7 %gather_fusion = bf16[64,512,128]{1,2,0:T(8,128)(2,1)} fusion(bf16[32,512,128]{1,2,0:T(8,128)(2,1)} %fusion, s32[1024]{0:T(1024)S(1)} %pad_clamp_fusion.5), kind=kCustom, calls=%fused_computation | custom fusion | bytes 16777472 | tf_op jit(solution)/shard_map/gather | solution.py:65
  223.5 6.2 copy.24
  229.7 4.3 gather_fusion.7
  239.9 4.4 gather_fusion.4
  244.2 322.4 %all-to-all-done.1 = bf16[8,16,512,128]{2,3,1,0:T(8,128)(2,1)} async-done(((bf16[8,16,512,128]{2,3,1,0:T(8,128)(2,1)}), bf16[8,16,512,128]{2,3,1,0:T(8,128)(2,1)}, u32[]{:S(2)}, u32[]{:S(2)}) %all-to-all-start.1) | async-done | bytes 16777248 | tf_op jit(solution)/shard_map/all_to_all | solution.py:76
  566.6 21.5 %copy.21 = bf16[8,16,512,128]{3,2,1,0:T(8,128)(2,1)} copy(bf16[8,16,512,128]{2,3,1,0:T(8,128)(2,1)} %all-to-all-done.1) | data formatting | bytes 33554432 | tf_op jit(solution)/shard_map/all_to_all | solution.py:76
  588.1 11.3 %gather_fusion.2 = bf16[64,512,128]{2,1,0:T(8,128)(2,1)} fusion(bf16[128,512,128]{2,1,0:T(8,128)(2,1)} %bitcast.53, s32[1024]{0:T(1024)S(1)} %pad_clamp_fusion.3), kind=kCustom, calls=%fused_computation.2 | custom fusion | bytes 16777472 | tf_op jit(solution)/shard_map/gather | solution.py:79
  599.4 8.1 %fusion.29 = bf16[64,128,128]{2,1,0:T(8,128)(2,1)S(1)} fusion(bf16[64,512,128]{1,2,0:T(8,128)(2,1)} %gather_fusion, bf16[64,512,128]{2,1,0:T(8,128)(2,1)} %gather_fusion.2), kind=kOutput, calls=%fused_computation.64 | convolution fusion | flops 1073741824 | bytes 18874368 | tf_op jit(solution)/shard_map/tkp,tkq->tpq/dot_general | solution.py:23
  607.5 5.7 convolution_multiply_fusion
  613.2 7.0 %add_negate_fusion = f32[32,128,128]{2,0,1:T(8,128)S(1)} fusion(f32[32,128,128]{2,0,1:T(8,128)} %fusion.10, f32[64,128,128]{2,1,0:T(8,128)} %convolution_multiply_fusion, s32[64]{0:T(128)S(1)} %copy-done.3), kind=kOutput, calls=%fused_computation.18 | convolution fusion | flops 403703808 | bytes 8388864 | tf_op jit(solution)/shard_map/at,tps->aps/dot_general | solution.py:41
  (53 shorter events, 30.5 us)
Async XLA Ops:
  0.0 203.1 %copy-start = (bf16[512,512]{1,0:T(8,128)(2,1)S(1)}, bf16[512,512]{1,0:T(8,128)(2,1)}, u32[]{:S(2)}) copy-start(bf16[512,512]{1,0:T(8,128)(2,1)} %param.15) | copy-start | bytes 1572868
  3.7 11.6 %all-to-all-start.3 = ((s32[4,1,8]{2,1,0:T(1,128)}), s32[4,1,8]{2,1,0:T(1,128)S(1)}, u32[]{:S(2)}, u32[]{:S(2)}) async-start(s32[4,1,8]{2,1,0:T(1,128)} %bitcast.16), calls=%async_computation.3 | async-start | bytes 4096 | tf_op jit(solution)/shard_map/all_to_all | solution.py:85
  15.3 10.4 %all-to-all-start = ((s32[8,1,16]{2,1,0:T(1,128)}), s32[8,1,16]{2,1,0:T(1,128)S(1)}, u32[]{:S(2)}, u32[]{:S(2)}) async-start(s32[8,1,16]{2,1,0:T(1,128)} %bitcast.6), calls=%async_computation | async-start | bytes 8192 | tf_op jit(solution)/shard_map/all_to_all | solution.py:69
  25.8 19.4 %all-to-all-start.5 = ((bf16[4,8,128,128]{3,2,1,0:T(8,128)(2,1)}), bf16[4,8,128,128]{3,2,1,0:T(8,128)(2,1)S(1)}, u32[]{:S(2)}, u32[]{:S(2)}) async-start(bf16[4,8,128,128]{3,2,1,0:T(8,128)(2,1)} %bitcast.20), calls=%async_computation.5 | async-start | bytes 2097152 | tf_op jit(solution)/shard_map/all_to_all | solution.py:93
  45.2 1.0 copy-start.2
  46.2 52.3 %all-to-all-start.4 = ((bf16[4,8,512,128]{2,3,1,0:T(8,128)(2,1)}), bf16[4,8,512,128]{2,3,1,0:T(8,128)(2,1)}, u32[]{:S(2)}, u32[]{:S(2)}) async-start(bf16[4,8,512,128]{2,3,1,0:T(8,128)(2,1)} %bitcast.54), calls=%async_computation.4 | async-start | bytes 8388608 | tf_op jit(solution)/shard_map/all_to_all | solution.py:92
  98.5 98.6 %all-to-all-start.2 = ((bf16[8,16,128,128]{3,2,1,0:T(8,128)(2,1)}), bf16[8,16,128,128]{3,2,1,0:T(8,128)(2,1)}, u32[]{:S(2)}, u32[]{:S(2)}) async-start(bf16[8,16,128,128]{3,2,1,0:T(8,128)(2,1)} %bitcast.55), calls=%async_computation.2 | async-start | bytes 8388608 | tf_op jit(solution)/shard_map/all_to_all | solution.py:77
  197.0 6.1 copy-start.3
  197.0 369.6 %all-to-all-start.1 = ((bf16[8,16,512,128]{2,3,1,0:T(8,128)(2,1)}), bf16[8,16,512,128]{2,3,1,0:T(8,128)(2,1)}, u32[]{:S(2)}, u32[]{:S(2)}) async-start(bf16[8,16,512,128]{2,3,1,0:T(8,128)(2,1)} %bitcast.52), calls=%async_computation.1 | async-start | bytes 33554432 | tf_op jit(solution)/shard_map/all_to_all | solution.py:76
  211.0 7.7 %copy-start.5 = (s32[16]{0:T(128)S(1)}, s32[16]{0:T(128)}, u32[]{:S(2)}) copy-start(s32[16]{0:T(128)} %param.22) | copy-start | bytes 196
  229.7 6.6 %copy-start.4 = (f32[16]{0:T(128)S(1)}, f32[16]{0:T(128)}, u32[]{:S(2)}) copy-start(f32[16]{0:T(128)} %param.23) | copy-start | bytes 196
  599.4 8.1 %copy-start.6 = (f32[64]{0:T(128)S(1)}, f32[64]{0:T(128)}, u32[]{:S(2)}) copy-start(f32[64]{0:T(128)} %param.19) | copy-start | bytes 772
  613.2 9.5 %copy-start.1 = (bf16[512,512]{1,0:T(8,128)(2,1)S(1)}, bf16[512,512]{1,0:T(8,128)(2,1)}, u32[]{:S(2)}) copy-start(bf16[512,512]{1,0:T(8,128)(2,1)} %param.15) | copy-start | bytes 1572868
where the time goes:
time: 624 us; the launch traced here: 623 us
  waiting for transfers between devices  453 us (73%)
  local copies, waits for them, and re-layouts  93.5 us (15%)
  matrix products  34.4 us (6%)
  starting transfers between devices  29.7 us (5%)
  other arithmetic  12.3 us (2%)
    all_to_all x1, waiting for transfers between devices, shards(): lax.all_to_all(sent_pno, 'mem', split_axis=0, concat_axis=0, tiled=True)  322 us
    all_to_all x1, waiting for transfers between devices, shards(): lax.all_to_all(sent_amp, 'mem', split_axis=0, concat_axis=0, tiled=True)  83.9 us
    all_to_all x1, waiting for transfers between devices, shards(): lax.all_to_all(out_pno, 'grp', split_axis=0, concat_axis=0, tiled=True)  43.6 us
    all_to_all x1, local copies, waits for them, and re-layouts, shards(): lax.all_to_all(sent_pno, 'mem', split_axis=0, concat_axis=0, tiled=True)  21.5 us
  transfers between devices with their start and end apart: 6, of which 4 were waited for; matrix products, arithmetic and copies ran while one was open for 13% of the time, Pallas kernels for 0%

commit v1 on v0

v1 whole, which is shorter than its diff:
```python
import functools

import jax
import jax.numpy as jnp
from jax import lax
from jax.experimental import pallas as pl
from jax.experimental.pallas import tpu as pltpu
from jax.sharding import PartitionSpec as P

UNIT = 16
ROUNDS = 10
SIZES = (24, 27, 30, 34)
VMEM = 48 * 2**20
ROW_BITS = 20
ANY = pl.BlockSpec(memory_space=pl.ANY)
SMEM = pl.BlockSpec(memory_space=pltpu.SMEM)
IN_VMEM = pl.BlockSpec(memory_space=pltpu.VMEM)


def params():
    return pltpu.CompilerParams(vmem_limit_bytes=VMEM)


def block_kernel(count_ref, pno_ref, amp_ref, out_ref):
    step = pl.program_id(0)
    many, depth, width = pno_ref.shape
    for i in range(many):
        count = count_ref[step * many + i]
        rows = lax.broadcasted_iota(jnp.int32, (width, depth), 0)
        turned = pno_ref[i].T
        out_ref[pl.ds(i * width, width), pl.ds(0, depth)] = jnp.where(rows < count, turned, jnp.zeros_like(turned))
        down = lax.broadcasted_iota(jnp.int32, (width, width), 0)
        across = lax.broadcasted_iota(jnp.int32, (width, width), 1)
        amp = amp_ref[i]
        live = (down < count) & (across < count)
        out_ref[pl.ds(i * width, width), pl.ds(depth, width)] = jnp.where(live, amp, jnp.zeros_like(amp))


def blocks_of(pno, amplitudes, pno_count):
    pairs, depth, width = pno.shape
    many = 4
    return pl.pallas_call(
        block_kernel,
        grid=(pairs // many,),
        in_specs=[
            SMEM,
            pl.BlockSpec((many, depth, width), lambda i: (i, 0, 0)),
            pl.BlockSpec((many, width, width), lambda i: (i, 0, 0)),
        ],
        out_specs=pl.BlockSpec((many * width, depth + width), lambda i: (i, 0)),
        out_shape=jax.ShapeDtypeStruct((pairs * width, depth + width), pno.dtype),
        compiler_params=params(),
    )(pno_count, pno, amplitudes)


def pick(array, index):
    return lax.dynamic_index_in_dim(array, index, 0, keepdims=False)


def starts_of(lengths, chips, delay):
    starts, ends = {}, []
    for c in range(chips - 1):
        at = jnp.zeros_like(lengths[0][chips - 1])
        for f in range(chips - 1, c, -1):
            for o in range(c, -1, -1):
                if o < c:
                    at = jnp.where(lengths[o][f] > 0, jnp.maximum(at, starts[o, f, c - 1] + delay), at)
                starts[o, f, c] = at
                at = at + lengths[o][f]
        ends.append(at)
    return starts, functools.reduce(jnp.maximum, ends)


def relay_plan(code, count, group, member, mine):
    groups, members, _ = code.shape
    pairs = count.shape[2]
    chips, items = members // 2, 2 * pairs
    chip, core = member // 2, member % 2
    ids = jnp.arange(members * pairs, dtype=jnp.int32)
    asked = jnp.any(code[..., None, :] == ids[:, None], axis=-1)
    asked = jnp.any(asked.reshape(groups, chips, 2, chips, items), axis=2)
    asked = jnp.stack([asked, asked[:, ::-1, ::-1]])
    line = jnp.arange(chips, dtype=jnp.int32)
    later = (line[:, None] > line[None, :])[:, :, None]
    far = jnp.max(jnp.where(asked & later, line[:, None, None], 0), axis=2)
    units = ((count + UNIT - 1) // UNIT).reshape(groups, chips, items)
    units = jnp.stack([units, units[:, ::-1]])
    order = far * items + (items - 1 - jnp.arange(items, dtype=jnp.int32))
    before = (order[..., None, :] > order[..., :, None]) & (far[..., None, :] > 0)
    lane = jnp.sum(before.astype(jnp.int32), axis=-1) & 1
    kind = far * 2 + lane
    ahead = before & (kind[..., None, :] == kind[..., :, None])
    prefix = jnp.sum(jnp.where(ahead, units[..., None, :], 0), axis=-1)
    kinds = jnp.arange(2 * chips, dtype=jnp.int32)
    total = jnp.sum(jnp.where(kind[..., None, :] == kinds[:, None], units[..., None, :], 0), axis=-1)
    total = total.reshape(2, groups, chips, chips, 2)
    lengths = [[total[:, :, o, f] for f in range(chips)] for o in range(chips)]
    branch, size = jnp.int32(len(SIZES)), jnp.int32(SIZES[-1])
    for b in range(len(SIZES) - 1, -1, -1):
        fits = jnp.max(starts_of(lengths, chips, 2 * SIZES[b])[1]) <= ROUNDS * SIZES[b]
        branch, size = jnp.where(fits, b, branch), jnp.where(fits, SIZES[b], size)

    def own_group(x):
        return lax.dynamic_index_in_dim(x, group, 1, keepdims=False)

    far, lane, prefix, units, total = (own_group(x) for x in (far, lane, prefix, units, total))
    lengths = [[total[:, o, f] for f in range(chips)] for o in range(chips)]
    starts = starts_of(lengths, chips, 2 * size)[0]
    none = jnp.zeros_like(lengths[0][0])
    runs = []
    most = max(c * (chips - 1 - c) for c in range(chips))
    for c in range(chips):
        own = [(starts[c, f, c], lengths[c][f], none) if f > c else (none, none, none) for f in range(1, chips)]
        passed = [(starts[o, f, c], lengths[o][f], starts[o, f, c - 1]) for o in range(c) for f in range(c + 1, chips)]
        passed += [(none, none, none)] * (most - len(passed))
        runs.append(jnp.stack([jnp.stack(r) for r in own + passed]))
    runs = jnp.stack(runs)
    outgo = jnp.stack([jnp.stack([starts[c, f, c] if f > c else none for f in range(chips)]) for c in range(chips)])
    income = jnp.stack(
        [
            jnp.stack([jnp.stack([starts[o, f, c - 1] if o < c <= f else none for f in range(chips)]) for o in range(chips)])
            for c in range(chips)
        ]
    )
    table, place, need, spot, side = [], [], [], [], []
    for d in range(2):
        at = chip if d == 0 else chips - 1 - chip
        table.append(lax.dynamic_index_in_dim(pick(runs, at)[..., d, :], core, 2, keepdims=False))
        home = pick(far[d], at)
        chosen = lax.dynamic_index_in_dim(pick(outgo, at)[:, d, :], core, 1, keepdims=False)
        first = jnp.sum(jnp.where(home[:, None] == line, chosen, 0), axis=1)
        place.append(first + pick(prefix[d], at))
        need.append(jnp.where((home > 0) & (pick(lane[d], at) == core), pick(units[d], at), 0))
        came = pick(income, at)[:, :, d, :]
        hit = (far[d][:, :, None, None] == line[:, None]) & (lane[d][:, :, None, None] == jnp.arange(2, dtype=jnp.int32))
        where = prefix[d] + jnp.sum(jnp.where(hit, came[:, None], 0), axis=(2, 3))
        spot.append(where if d == 0 else where[::-1])
        side.append(lane[d] if d == 0 else lane[d][::-1])
    stretch = ROUNDS * size + 8
    origin = line[:, None]
    item = jnp.arange(items, dtype=jnp.int32)[None, :]
    width = mine[1]
    down = (origin > chip).astype(jnp.int32)
    lies = jnp.where(down == 1, spot[1], spot[0])
    on = jnp.where(down == 1, side[1], side[0])
    far_row = ((2 * down + (on != core)) * stretch + lies) * UNIT + (2 << ROW_BITS)
    near_row = (item % pairs) * width + ((item // pairs != core).astype(jnp.int32) << ROW_BITS)
    rows = jnp.where(origin == chip, near_row, far_row).reshape(-1)
    location = jnp.sum(jnp.where(mine[0][:, None] == ids, rows, 0), axis=1)
    return branch, jnp.stack(table), jnp.stack(place), jnp.stack(need), location


def ranks_of(owner):
    spots = jnp.arange(owner.shape[-1], dtype=jnp.int32)
    ahead = (owner[..., None, :] == owner[..., :, None]) & (spots[None, :] < spots[:, None])
    return jnp.sum(ahead.astype(jnp.int32), axis=-1)


def wanted_from(owner, pair, me, capacity):
    slot = jnp.where(owner == me, ranks_of(owner), capacity)
    hit = slot[:, None, :] == jnp.arange(capacity, dtype=jnp.int32)[:, None]
    return jnp.sum(jnp.where(hit, pair[:, None, :], 0), axis=-1)


def take_kernel(width, depth, index_ref, blocks_ref, *refs):
    outs, sem = refs[:-1], refs[-1]
    slots = outs[0].shape[0] // width

    def copies(i):
        for k, out in enumerate(outs):
            row = pl.multiple_of(index_ref[k * slots + i] * width, UNIT)
            yield pltpu.make_async_copy(
                blocks_ref.at[pl.ds(row, width)], out.at[pl.ds(pl.multiple_of(i * width, UNIT), width)], sem
            )

    @pl.loop(0, slots)
    def _(i):
        for c in copies(i):
            c.start()

    @pl.loop(0, slots)
    def _(i):
        for c in copies(i):
            c.wait()


def take(blocks, index, width, parts):
    slots = index.shape[0] // parts
    shape = jax.ShapeDtypeStruct((slots * width, blocks.shape[1]), blocks.dtype)
    return pl.pallas_call(
        functools.partial(take_kernel, width, blocks.shape[1]),
        in_specs=[SMEM, ANY],
        out_specs=[ANY] * parts,
        out_shape=[shape] * parts,
        scratch_shapes=[pltpu.SemaphoreType.DMA],
        compiler_params=params(),
        cost_estimate=pl.CostEstimate(flops=0, bytes_accessed=2 * parts * slots * width * blocks.shape[1] * 2, transcendentals=0),
    )(index, blocks)


def run_copies(runs_ref, d, r, window, size, source, out, sem, shift):
    first, length, back = runs_ref[d, r, 0], runs_ref[d, r, 1], runs_ref[d, r, 2]
    low = jnp.maximum(first, window * size)
    high = jnp.minimum(first + length, (window + 1) * size)
    taken = jnp.maximum(high - low, 0)
    begin = back + low - first if shift else low
    rows = taken * UNIT
    return taken, pltpu.make_async_copy(
        source.at[d, pl.ds(pl.multiple_of(jnp.maximum(begin, 0) * UNIT, UNIT), rows)],
        out.at[pl.ds(pl.multiple_of((low - window * size) * UNIT, UNIT), rows)],
        sem,
    )


def windows(runs_ref, picks, window, size, source, outs, sem, shift, act):
    for d in range(2):
        for r in picks:
            taken, copy = run_copies(runs_ref, d, r, window, size, source, outs[d], sem, shift)

            @pl.when(taken > 0)
            def _():
                getattr(copy, act)()


def open_kernel(size, pairs, width, own, place_ref, need_ref, runs_ref, core_ref, mine_ref, other_ref, stream_ref, *refs):
    outs, sem = refs[:-1], refs[-1]

    def each(act):
        for half, source in ((0, mine_ref), (1, other_ref)):

            @pl.loop(0, pairs)
            def _(i):
                for d in range(2):
                    item = (core_ref[0] ^ half) * pairs + i
                    units = need_ref[d, item]
                    rows = units * UNIT

                    @pl.when(units > 0)
                    def _():
                        copy = pltpu.make_async_copy(
                            source.at[pl.ds(pl.multiple_of(i * width, UNIT), rows)],
                            stream_ref.at[d, pl.ds(pl.multiple_of(place_ref[d, item] * UNIT, UNIT), rows)],
                            sem,
                        )
                        getattr(copy, act)()

    each("start")
    each("wait")
    for act in ("start", "wait"):
        for window in range(2):
            windows(runs_ref, range(own), window, size, stream_ref, outs[2 * window : 2 * window + 2], sem, False, act)


def step_kernel(size, stretch, number, sends, own, runs_ref, stream_ref, *refs):
    refs = list(refs)
    held = refs.pop(0) if number > 0 else None
    came = [refs.pop(0), refs.pop(0)]
    other = [refs.pop(0), refs.pop(0)] if number > 0 else []
    del held
    hold = refs.pop(0)
    outs = [refs.pop(0), refs.pop(0)] if sends else []
    arrive, rest, lay = refs
    rows = size * UNIT
    first = [
        pltpu.make_async_copy(came[d], hold.at[2 * d, pl.ds(number * rows, rows)], arrive.at[d]) for d in range(2)
    ]
    second = [
        pltpu.make_async_copy(other[d], hold.at[2 * d + 1, pl.ds((number - 1) * rows, rows)], rest.at[d])
        for d in range(2)
        if other
    ]
    for c in first + second:
        c.start()
    if sends:
        windows(runs_ref, range(own), number + 2, size, stream_ref, outs, lay, False, "start")
        windows(runs_ref, range(own), number + 2, size, stream_ref, outs, lay, False, "wait")
    for c in first:
        c.wait()
    if sends:
        for act in ("start", "wait"):
            for d in range(2):
                for r in range(own, runs_ref.shape[1]):
                    taken, copy = run_copies(runs_ref, d, r, number + 2, size, hold.at[pl.ds(d, 2)], outs[d], lay, True)

                    @pl.when(taken > 0)
                    def _():
                        getattr(copy, act)()
    for c in second:
        c.wait()


def close_kernel(size, number, came_up, came_down, held_ref, hold, sem):
    del held_ref
    rows = size * UNIT
    copies = [
        pltpu.make_async_copy(c, hold.at[2 * d + 1, pl.ds(number * rows, rows)], sem.at[d])
        for d, c in enumerate((came_up, came_down))
    ]
    for c in copies:
        c.start()
    for c in copies:
        c.wait()


def couple_kernel(tasks, width, depth, many, loc_ref, count_ref, target_ref, coef_ref, metric_ref, *refs):
    out_ref, slots, sems = refs[-3], refs[-2], refs[-1]
    buffers = refs[:-3]
    out_ref[...] = jnp.zeros_like(out_ref)

    def fetch(group, phase):
        for u in range(many):
            code = loc_ref[group * many + u]
            row = pl.multiple_of(code & ((1 << ROW_BITS) - 1), UNIT)
            for b, source in enumerate(buffers):

                @pl.when((code >> ROW_BITS) == b)
                def _():
                    pltpu.make_async_copy(source.at[pl.ds(row, width)], slots.at[phase, u], sems.at[phase, u]).start()

    groups = tasks // many
    fetch(0, 0)

    @pl.loop(0, groups)
    def _(group):
        phase = lax.rem(group, 2)

        @pl.when(group + 1 < groups)
        def _():
            fetch(group + 1, 1 - phase)

        terms = []
        for u in range(many):
            pltpu.make_async_copy(buffers[0].at[pl.ds(0, width)], slots.at[phase, u], sems.at[phase, u]).wait()
        for u in range(many):
            t = group * many + u
            held = slots[phase, u]
            rows = lax.broadcasted_iota(jnp.int32, held.shape, 0)
            held = jnp.where(rows < count_ref[t], held, jnp.zeros_like(held))
            turned = lax.dot_general(
                held[:, :depth], metric_ref[target_ref[t]], (((1,), (1,)), ((), ())), preferred_element_type=jnp.float32
            ).astype(jnp.bfloat16)
            half = lax.dot_general(
                turned, held[:, depth:], (((0,), (0,)), ((), ())), preferred_element_type=jnp.float32
            ).astype(jnp.bfloat16)
            terms.append(coef_ref[t] * jnp.dot(half, turned, preferred_element_type=jnp.float32))
        for u in range(many):
            target = target_ref[group * many + u]
            out_ref[target] = out_ref[target] - terms[u]


def couple(location, count, target, coef, metric, buffers, width, depth):
    tasks, pairs = location.shape[0], metric.shape[0]
    many = 4
    return pl.pallas_call(
        functools.partial(couple_kernel, tasks, width, depth, many),
        in_specs=[SMEM] * 4 + [IN_VMEM] + [ANY] * len(buffers),
        out_specs=IN_VMEM,
        out_shape=jax.ShapeDtypeStruct((pairs, width, width), jnp.float32),
        scratch_shapes=[
            pltpu.VMEM((2, many, width, depth + width), jnp.bfloat16),
            pltpu.SemaphoreType.DMA((2, many)),
        ],
        compiler_params=params(),
    )(location, count, target, coef, metric, *buffers)


def relay(size, chips, pairs, width, table, place, need, core, mine, other):
    columns = mine.shape[1]
    stretch = ROUNDS * size + 8
    own = chips - 1
    piece = jax.ShapeDtypeStruct((size * UNIT, columns), mine.dtype)
    stream_shape = jax.ShapeDtypeStruct((2, ROUNDS * size * UNIT, columns), mine.dtype)
    hold_shape = jax.ShapeDtypeStruct((4, stretch * UNIT, columns), mine.dtype)
    members = 2 * chips
    ways = [
        [(i, i + 2) for i in range(members - 2)],
        [(i + 2, i) for i in range(members - 2)],
    ]
    across = [(i, i ^ 1) for i in range(members)]
    stream, *opened = pl.pallas_call(
        functools.partial(open_kernel, size, pairs, width, own),
        in_specs=[SMEM] * 4 + [ANY] * 2,
        out_specs=[ANY] * 5,
        out_shape=[stream_shape] + [piece] * 4,
        scratch_shapes=[pltpu.SemaphoreType.DMA],
        compiler_params=params(),
    )(place, need, table, core, mine, other)
    sends = [opened[:2], opened[2:]]
    hold, swapped = None, None
    for number in range(ROUNDS):
        came = [lax.ppermute(sends[number][d], "mem", ways[d]) for d in range(2)]
        ends = number + 2 >= ROUNDS
        operands = [table, stream] + ([hold] if number else []) + came + (swapped if number else [])
        results = pl.pallas_call(
            functools.partial(step_kernel, size, stretch, number, not ends, own),
            in_specs=[SMEM] + [ANY] * (len(operands) - 1),
            out_specs=[ANY] * (1 if ends else 3),
            out_shape=[hold_shape] + ([] if ends else [piece] * 2),
            input_output_aliases={2: 0} if number else {},
            scratch_shapes=[pltpu.SemaphoreType.DMA((2,)), pltpu.SemaphoreType.DMA((2,)), pltpu.SemaphoreType.DMA],
            compiler_params=params(),
            cost_estimate=pl.CostEstimate(flops=0, bytes_accessed=12 * size * UNIT * columns * 2, transcendentals=0),
        )(*operands)
        hold = results[0]
        sends.append(results[1:])
        swapped = [lax.ppermute(came[d], "mem", across) for d in range(2)]
    return pl.pallas_call(
        functools.partial(close_kernel, size, ROUNDS - 1),
        in_specs=[ANY] * 3,
        out_specs=ANY,
        out_shape=hold_shape,
        input_output_aliases={2: 0},
        scratch_shapes=[pltpu.SemaphoreType.DMA((2,))],
        compiler_params=params(),
    )(*swapped, hold)


def shards(
    pno,
    amplitudes,
    pno_count,
    pao_coupling,
    row_owner,
    row_pair,
    row_target,
    row_coef,
    column_owner,
    column_pair,
    column_target,
    column_coef,
):
    pairs, depth, width = pno.shape
    tasks, crossings = row_pair.shape[0], column_pair.shape[0]
    members, groups = lax.axis_size("mem"), lax.axis_size("grp")
    member, group = lax.axis_index("mem"), lax.axis_index("grp")
    row_cap = max(2, 2 * tasks // members)
    col_cap = max(2, 2 * crossings // groups)
    chips = members // 2
    row_owner, column_owner = row_owner[:, 0], column_owner[:, 0]
    row_code = row_owner * pairs + row_pair
    col_code = column_owner * pairs + column_pair
    told = lax.all_gather(jnp.concatenate([row_code, col_code, pno_count]), ("grp", "mem"))
    told = told.reshape(groups, members, -1)
    code, cols, count = told[..., :tasks], told[..., tasks : tasks + crossings], told[..., tasks + crossings :]
    blocks = blocks_of(pno, amplitudes, pno_count)
    metric = blocks[:, :depth].astype(jnp.float32) + jnp.dot(
        blocks[:, :depth], pao_coupling, preferred_element_type=jnp.float32
    )
    metric = metric.astype(jnp.bfloat16).reshape(pairs, width, depth)
    ids = jnp.arange(members * pairs, dtype=jnp.int32)
    here = pick(count, group).reshape(-1)
    row_count = jnp.sum(jnp.where(row_code[:, None] == ids, here, 0), axis=1)
    beside = lax.dynamic_index_in_dim(count, member, 1, keepdims=False).reshape(-1)
    col_ids = jnp.arange(groups * pairs, dtype=jnp.int32)
    col_count = jnp.sum(jnp.where(col_code[:, None] == col_ids, beside, 0), axis=1)
    ask = lax.dynamic_index_in_dim(cols, member, 1, keepdims=False)
    asked = wanted_from(ask // pairs, ask % pairs, group, col_cap)
    shifts = range(1, groups)
    index = jnp.concatenate([pick(asked, (group + k) % groups) for k in shifts])
    step = (group - column_owner) % groups
    col_row = (ranks_of(column_owner) + 0) * width
    target = jnp.concatenate([row_target, column_target])
    coef = jnp.concatenate([row_coef, column_coef])
    counts = jnp.concatenate([row_count, col_count])

    def crossed():
        parts = take(blocks, index, width, groups - 1)
        return [
            lax.ppermute(parts[k - 1], "grp", [(g, (g + k) % groups) for g in range(groups)]) for k in shifts
        ]

    def finish(location, buffers):
        from_own = column_pair * width
        first = len(buffers)
        col_location = jnp.where(step == 0, from_own, col_row + ((first + step - 1) << ROW_BITS))
        return couple(
            jnp.concatenate([location, col_location]), counts, target, coef, metric, buffers + crossed(), width, depth
        )

    def plain(*_):
        want = wanted_from(pick(code, group) // pairs, pick(code, group) % pairs, member, row_cap)
        [sent] = take(blocks, want.reshape(-1), width, 1)
        got = lax.all_to_all(sent, "mem", split_axis=0, concat_axis=0, tiled=True)
        location = (row_owner * row_cap + ranks_of(row_owner)) * width + (1 << ROW_BITS)
        return finish(location, [blocks, got])

    if members % 2 or chips < 2 or chips > 4:
        return plain()
    other = lax.ppermute(blocks, "mem", [(i, i ^ 1) for i in range(members)])
    branch, table, place, need, location = relay_plan(code, count, group, member, (row_code, width))
    core = (member % 2).reshape(1).astype(jnp.int32)

    def relayed(size, table, place, need, location, other):
        hold = relay(size, chips, pairs, width, table, place, need, core, blocks, other)
        return finish(location, [blocks, other, hold.reshape(-1, hold.shape[2])])

    branches = [functools.partial(relayed, size) for size in SIZES] + [plain]
    return lax.switch(branch, branches, table, place, need, location, other)


def solution(mesh):
    in_specs = (
        P(("grp", "mem"), None, None),
        P(("grp", "mem"), None, None),
        P(("grp", "mem")),
        P(),
        P(("grp", "mem"), None),
        P(("grp", "mem")),
        P(("grp", "mem")),
        P(("grp", "mem")),
        P(("grp", "mem"), None),
        P(("grp", "mem")),
        P(("grp", "mem")),
        P(("grp", "mem")),
    )
    out_specs = P(("grp", "mem"), None, None)
    return jax.shard_map(shards, mesh=mesh, in_specs=in_specs, out_specs=out_specs, check_vma=False)
```

time: 624 us -> 658 us (1.054)
  the two profiles are of different devices: /device:TPU:0 before, /device:TPU:3 now
where the time goes in v1:
time: 658 us; the launch traced here: 650 us
  Pallas kernels  416 us (63%)
  starting transfers between devices  121 us (18%)
  blocking collectives  41 us (6%)
  waiting for transfers between devices  38.3 us (6%)
  local copies, waits for them, and re-layouts  14.1 us (2%)
  matrix products  7.82 us (1%)
  other arithmetic  7.38 us (1%)
    pallas_call x1, Pallas kernels, take(): pl.pallas_call(functools.partial(take_kernel, width, blocks.shape[1]), in...  121 us
    pallas_call x10, Pallas kernels, relay(): pl.pallas_call(functools.partial(step_kernel, size, stretch, number, not...  114 us
    pallas_call x1, Pallas kernels, relay(): pl.pallas_call(functools.partial(open_kernel, size, pairs, width, own), i...  103 us
    ppermute x20, starting transfers between devices, relay(): came = [lax.ppermute(sends[number][d], 'mem', ways[d]) for d in range(2)]  86.7 us
    unnamed x1, blocking collectives  41 us
    pallas_call x1, Pallas kernels, relay(): pl.pallas_call(functools.partial(close_kernel, size, ROUNDS - 1), in_spec...  38.3 us
    ppermute x20, waiting for transfers between devices, relay(): came = [lax.ppermute(sends[number][d], 'mem', ways[d]) for d in range(2)]  36.5 us
    pallas_call x1, Pallas kernels, couple(): pl.pallas_call(functools.partial(couple_kernel, tasks, width, depth, many...  34.6 us
  transfers between devices with their start and end apart: 44, of which 15 were waited for; matrix products, arithmetic and copies ran while one was open for 3% of the time, Pallas kernels for 42%

profile of v1, /device:TPU:3, one launch (start us, length us, event | category | flops | bytes accessed | tf_op | source)
XLA Modules:
  0.0 649.6 jit_solution(13147343131715802448)
XLA Ops:
  4.2 5.1 shard_map.123
  10.2 41.0 %all-reduce = s32[3584]{0:T(1024)S(1)} all-reduce(s32[3584]{0:T(1024)S(1)} %add_dynamic-update-slice_fusion), channel_id=2, replica_groups=mesh['grp'=4,'mem'=8] {'grp','mem'}, use_global_device_ids=true, to_apply=%add | all-reduce | flops 3584 | bytes 28672
  65.0 7.8 %add_convert_fusion = bf16[4096,512]{1,0:T(8,128)(2,1)} fusion(bf16[512,512]{1,0:T(8,128)(2,1)S(1)} %copy-done, bf16[4096,640]{1,0:T(8,128)(2,1)} %shard_map.123), kind=kOutput, calls=%fused_computation.103 | convolution fusion | flops 2153775104 | bytes 13107200 | tf_op jit(solution)/shard_map/dot_general | solution.py:446
  73.5 575.0 %conditional.1 = (f32[32,128,128]{2,1,0:T(8,128)}) conditional(s32[]{:T(128)} %clamp.3, (s32[]{:T(128)}, s32[4,1]{0,1:T(1,128)S(1)}, s32[1,64]{1,0:T(1,128)S(1)}, s32[1,64]{1,0:T(1,128)S(1)}, s32[1,64]{1,0:T(1,128)S(1)}, /*index=5*/s32[4,1]{0,1:T(1,128)S(1)}, s32[4,64]{1,0:T(4,128)S(1)}, s32[]{:T(128)}, ...), branch_computations={%region_18.21_spmd, %region_21.24_spmd, %region_24.27_spmd, %regio... | conditional | flops 193779 | bytes 247434144 | solution.py:498
  73.8 103.0 %branch_2_fun.14 = (bf16[2,4800,640]{2,1,0:T(8,128)(2,1)}, bf16[480,640]{1,0:T(8,128)(2,1)S(1)}, bf16[480,640]{1,0:T(8,128)(2,1)S(1)}, bf16[480,640]{1,0:T(8,128)(2,1)S(1)}, bf16[480,640]{1,0:T(8,128)(2,1)S(1)}) custom-call(s32[2,64]{1,0:T(2,128)S(1)} %get-tuple-element.777.place_ref, s32[2,64]{1,0:T(2,128)S(1)} %get-tuple-element.778.need_ref, ...), custom_call_target="tpu_custom_call" | custom-call | tf_op jit(solution)/shard_map/cond/branch_2_fun/pallas_call | solution.py:380
  176.8 36.6 %collective-permute-start.86 = (bf16[480,640]{1,0:T(8,128)(2,1)S(1)}, bf16[480,640]{1,0:T(8,128)(2,1)S(1)}, u32[]{:S(2)}, u32[]{:S(2)}) collective-permute-start(bf16[480,640]{1,0:T(8,128)(2,1)S(1)} %get-tuple-element.781), channel_id=1, source_target_pairs={{0,2},{1,3},{2,4},{3,5},{4,6},{5,7},{8,10},{9,11},{10,12},{11,13},... | collective-permute-start | bytes 1843208 | tf_op jit(solution)/shard_map/cond/branch_2_fun/ppermute | solution.py:391
  214.7 4.0 collective-permute-start.88
  220.4 13.6 %collective-permute-start.90 = (bf16[480,640]{1,0:T(8,128)(2,1)S(1)}, bf16[480,640]{1,0:T(8,128)(2,1)S(1)}, u32[]{:S(2)}, u32[]{:S(2)}) collective-permute-start(bf16[480,640]{1,0:T(8,128)(2,1)S(1)} %collective-permute-done.86.refs_0_), channel_id=1, source_target_pairs={{0,1},{1,0},{2,3},{3,2},{4,5},{5,4},{6,7},{7,6},{8,9},{9,8},{10,11... | collective-permute-start | bytes 1843208 | tf_op jit(solution)/shard_map/cond/branch_2_fun/ppermute | solution.py:406
  234.0 4.1 collective-permute-start.91
  247.6 4.8 collective-permute-start.96
  252.4 4.2 collective-permute-done.92.refs_1_
  263.9 3.1 collective-permute-start.100
  277.7 4.3 collective-permute-start.104
  290.9 4.6 collective-permute-start.108
  304.0 4.3 collective-permute-start.112
  317.2 4.1 collective-permute-start.120
  321.3 120.8 %branch_2_fun.26 = (bf16[1024,640]{1,0:T(8,128)(2,1)}, bf16[1024,640]{1,0:T(8,128)(2,1)}, bf16[1024,640]{1,0:T(8,128)(2,1)}) custom-call(s32[24]{0:T(128)S(1)} %get-tuple-element.809.index_ref, bf16[4096,640]{1,0:T(8,128)(2,1)} %get-tuple-element.774.mine_ref.blocks_ref.refs_0_), custom_call_target="tpu_custom_call" | custom-call | bytes 7864320 | tf_op jit(solution)/shard_map/cond/branch_2_fun/pallas_call | solution.py:190
  446.5 5.1 collective-permute-start.116
  453.0 5.7 collective-permute-done.121.refs_2_
  465.4 6.4 collective-permute-done.118.refs_2_
  478.4 20.4 %branch_2_fun.23.refs_0_ = bf16[4,4928,640]{2,1,0:T(8,128)(2,1)} custom-call(s32[2,5,3]{2,1,0:T(8,128)S(1)} %copy.195.runs_ref, bf16[2,4800,640]{2,1,0:T(8,128)(2,1)} %get-tuple-element.780.stream_ref, bf16[4,4928,640]{2,1,0:T(8,128)(2,1)} %get-tuple-element.806.refs_0_, ...), custom_call_target="tpu_custom_call", output_to_operand_aliasing={{}: (2, {})} | custom-call | bytes 7372800 | tf_op jit(solution)/shard_map/cond/branch_2_fun/pallas_call | solution.py:394
  498.8 76.3 %branch_2_fun.24.held_ref = bf16[4,4928,640]{2,1,0:T(8,128)(2,1)} custom-call(s32[2,5,3]{2,1,0:T(8,128)S(1)} %copy.195.runs_ref, bf16[2,4800,640]{2,1,0:T(8,128)(2,1)} %get-tuple-element.780.stream_ref, bf16[4,4928,640]{2,1,0:T(8,128)(2,1)} %branch_2_fun.23.refs_0_, ...), custom_call_target="tpu_custom_call", output_to_operand_aliasing={{}: (2, {})} | custom-call | bytes 7372800 | tf_op jit(solution)/shard_map/cond/branch_2_fun/pallas_call | solution.py:394
  575.1 38.3 %branch_2_fun.25 = bf16[4,4928,640]{2,1,0:T(8,128)(2,1)} custom-call(bf16[480,640]{1,0:T(8,128)(2,1)} %collective-permute-done.117.came_up, bf16[480,640]{1,0:T(8,128)(2,1)} %collective-permute-done.119.came_down, bf16[4,4928,640]{2,1,0:T(8,128)(2,1)} %branch_2_fun.24.held_ref), custom_call_target="tpu_custom_call", output_to_operand_aliasing={{}: (2, {})} | custom-call | tf_op jit(solution)/shard_map/cond/branch_2_fun/pallas_call | solution.py:407
  613.5 34.6 %branch_2_fun.27 = f32[32,128,128]{2,1,0:T(8,128)} custom-call(s32[80]{0:T(128)S(1)} %pad_add_fusion.2.loc_ref, s32[80]{0:T(128)S(1)} %get-tuple-element.770.count_ref, s32[80]{0:T(128)S(1)} %get-tuple-element.771.target_ref, f32[80]{0:T(128)S(1)} %get-tuple-element.772.coef_ref, bf16[32,128,512]{2,1,0:T(8,128)(2,1)S(1)} %copy-done.34, ...), custom_call_target="tpu_custom_call" | custom-call | tf_op jit(solution)/shard_map/cond/branch_2_fun/pallas_call | solution.py:354
  (284 shorter events, 93.3 us)
Async XLA Ops:
  9.2 64.1 %collective-permute-start.175 = (bf16[4096,640]{1,0:T(8,128)(2,1)}, bf16[4096,640]{1,0:T(8,128)(2,1)}, u32[]{:S(2)}, u32[]{:S(2)}) collective-permute-start(bf16[4096,640]{1,0:T(8,128)(2,1)} %shard_map.123), channel_id=1, source_target_pairs={{0,1},{1,0},{2,3},{3,2},{4,5},{5,4},{6,7},{7,6},{8,9},{9,8},{10,11... | collective-permute-start | bytes 15728648 | tf_op jit(solution)/shard_map/ppermute | solution.py:489
  176.8 43.6 %collective-permute-start.86 = (bf16[480,640]{1,0:T(8,128)(2,1)S(1)}, bf16[480,640]{1,0:T(8,128)(2,1)S(1)}, u32[]{:S(2)}, u32[]{:S(2)}) collective-permute-start(bf16[480,640]{1,0:T(8,128)(2,1)S(1)} %get-tuple-element.781), channel_id=1, source_target_pairs={{0,2},{1,3},{2,4},{3,5},{4,6},{5,7},{8,10},{9,11},{10,12},{11,13},... | collective-permute-start | bytes 1843208 | tf_op jit(solution)/shard_map/cond/branch_2_fun/ppermute | solution.py:391
  213.4 20.6 %collective-permute-start.87 = (bf16[480,640]{1,0:T(8,128)(2,1)S(1)}, bf16[480,640]{1,0:T(8,128)(2,1)S(1)}, u32[]{:S(2)}, u32[]{:S(2)}) collective-permute-start(bf16[480,640]{1,0:T(8,128)(2,1)S(1)} %get-tuple-element.782), channel_id=1, source_target_pairs={{2,0},{3,1},{4,2},{5,3},{6,4},{7,5},{10,8},{11,9},{12,10},{13,11},... | collective-permute-start | bytes 1843208 | tf_op jit(solution)/shard_map/cond/branch_2_fun/ppermute | solution.py:391
  214.7 28.7 %collective-permute-start.88 = (bf16[480,640]{1,0:T(8,128)(2,1)S(1)}, bf16[480,640]{1,0:T(8,128)(2,1)S(1)}, u32[]{:S(2)}, u32[]{:S(2)}) collective-permute-start(bf16[480,640]{1,0:T(8,128)(2,1)S(1)} %get-tuple-element.784), channel_id=1, source_target_pairs={{0,2},{1,3},{2,4},{3,5},{4,6},{5,7},{8,10},{9,11},{10,12},{11,13},... | collective-permute-start | bytes 1843208 | tf_op jit(solution)/shard_map/cond/branch_2_fun/ppermute | solution.py:391
  218.7 26.0 %collective-permute-start.89 = (bf16[480,640]{1,0:T(8,128)(2,1)S(1)}, bf16[480,640]{1,0:T(8,128)(2,1)S(1)}, u32[]{:S(2)}, u32[]{:S(2)}) collective-permute-start(bf16[480,640]{1,0:T(8,128)(2,1)S(1)} %get-tuple-element.785), channel_id=1, source_target_pairs={{2,0},{3,1},{4,2},{5,3},{6,4},{7,5},{10,8},{11,9},{12,10},{13,11},... | collective-permute-start | bytes 1843208 | tf_op jit(solution)/shard_map/cond/branch_2_fun/ppermute | solution.py:391
  220.4 24.6 %collective-permute-start.90 = (bf16[480,640]{1,0:T(8,128)(2,1)S(1)}, bf16[480,640]{1,0:T(8,128)(2,1)S(1)}, u32[]{:S(2)}, u32[]{:S(2)}) collective-permute-start(bf16[480,640]{1,0:T(8,128)(2,1)S(1)} %collective-permute-done.86.refs_0_), channel_id=1, source_target_pairs={{0,1},{1,0},{2,3},{3,2},{4,5},{5,4},{6,7},{7,6},{8,9},{9,8},{10,11... | collective-permute-start | bytes 1843208 | tf_op jit(solution)/shard_map/cond/branch_2_fun/ppermute | solution.py:406
  247.6 22.2 %collective-permute-start.96 = (bf16[480,640]{1,0:T(8,128)(2,1)S(1)}, bf16[480,640]{1,0:T(8,128)(2,1)S(1)}, u32[]{:S(2)}, u32[]{:S(2)}) collective-permute-start(bf16[480,640]{1,0:T(8,128)(2,1)S(1)} %get-tuple-element.790), channel_id=1, source_target_pairs={{0,2},{1,3},{2,4},{3,5},{4,6},{5,7},{8,10},{9,11},{10,12},{11,13},... | collective-permute-start | bytes 1843208 | tf_op jit(solution)/shard_map/cond/branch_2_fun/ppermute | solution.py:391
  256.6 17.1 %collective-permute-start.97 = (bf16[480,640]{1,0:T(8,128)(2,1)S(1)}, bf16[480,640]{1,0:T(8,128)(2,1)S(1)}, u32[]{:S(2)}, u32[]{:S(2)}) collective-permute-start(bf16[480,640]{1,0:T(8,128)(2,1)S(1)} %get-tuple-element.791), channel_id=1, source_target_pairs={{2,0},{3,1},{4,2},{5,3},{6,4},{7,5},{10,8},{11,9},{12,10},{13,11},... | collective-permute-start | bytes 1843208 | tf_op jit(solution)/shard_map/cond/branch_2_fun/ppermute | solution.py:391
  263.9 19.0 %collective-permute-start.100 = (bf16[480,640]{1,0:T(8,128)(2,1)S(1)}, bf16[480,640]{1,0:T(8,128)(2,1)S(1)}, u32[]{:S(2)}, u32[]{:S(2)}) collective-permute-start(bf16[480,640]{1,0:T(8,128)(2,1)S(1)} %get-tuple-element.793), channel_id=1, source_target_pairs={{0,2},{1,3},{2,4},{3,5},{4,6},{5,7},{8,10},{9,11},{10,12},{11,13},... | collective-permute-start | bytes 1843208 | tf_op jit(solution)/shard_map/cond/branch_2_fun/ppermute | solution.py:391
  277.7 18.4 %collective-permute-start.104 = (bf16[480,640]{1,0:T(8,128)(2,1)S(1)}, bf16[480,640]{1,0:T(8,128)(2,1)S(1)}, u32[]{:S(2)}, u32[]{:S(2)}) collective-permute-start(bf16[480,640]{1,0:T(8,128)(2,1)S(1)} %get-tuple-element.796), channel_id=1, source_target_pairs={{0,2},{1,3},{2,4},{3,5},{4,6},{5,7},{8,10},{9,11},{10,12},{11,13},... | collective-permute-start | bytes 1843208 | tf_op jit(solution)/shard_map/cond/branch_2_fun/ppermute | solution.py:391
  283.0 17.1 %collective-permute-start.105 = (bf16[480,640]{1,0:T(8,128)(2,1)S(1)}, bf16[480,640]{1,0:T(8,128)(2,1)S(1)}, u32[]{:S(2)}, u32[]{:S(2)}) collective-permute-start(bf16[480,640]{1,0:T(8,128)(2,1)S(1)} %get-tuple-element.797), channel_id=1, source_target_pairs={{2,0},{3,1},{4,2},{5,3},{6,4},{7,5},{10,8},{11,9},{12,10},{13,11},... | collective-permute-start | bytes 1843208 | tf_op jit(solution)/shard_map/cond/branch_2_fun/ppermute | solution.py:391
  290.9 18.4 %collective-permute-start.108 = (bf16[480,640]{1,0:T(8,128)(2,1)S(1)}, bf16[480,640]{1,0:T(8,128)(2,1)S(1)}, u32[]{:S(2)}, u32[]{:S(2)}) collective-permute-start(bf16[480,640]{1,0:T(8,128)(2,1)S(1)} %get-tuple-element.799), channel_id=1, source_target_pairs={{0,2},{1,3},{2,4},{3,5},{4,6},{5,7},{8,10},{9,11},{10,12},{11,13},... | collective-permute-start | bytes 1843208 | tf_op jit(solution)/shard_map/cond/branch_2_fun/ppermute | solution.py:391
  296.1 17.1 %collective-permute-start.109 = (bf16[480,640]{1,0:T(8,128)(2,1)S(1)}, bf16[480,640]{1,0:T(8,128)(2,1)S(1)}, u32[]{:S(2)}, u32[]{:S(2)}) collective-permute-start(bf16[480,640]{1,0:T(8,128)(2,1)S(1)} %get-tuple-element.800), channel_id=1, source_target_pairs={{2,0},{3,1},{4,2},{5,3},{6,4},{7,5},{10,8},{11,9},{12,10},{13,11},... | collective-permute-start | bytes 1843208 | tf_op jit(solution)/shard_map/cond/branch_2_fun/ppermute | solution.py:391
  304.0 138.0 %collective-permute-start.112 = (bf16[480,640]{1,0:T(8,128)(2,1)S(1)}, bf16[480,640]{1,0:T(8,128)(2,1)S(1)}, u32[]{:S(2)}, u32[]{:S(2)}) collective-permute-start(bf16[480,640]{1,0:T(8,128)(2,1)S(1)} %get-tuple-element.802), channel_id=1, source_target_pairs={{0,2},{1,3},{2,4},{3,5},{4,6},{5,7},{8,10},{9,11},{10,12},{11,13},... | collective-permute-start | bytes 1843208 | tf_op jit(solution)/shard_map/cond/branch_2_fun/ppermute | solution.py:391
  309.3 134.1 %collective-permute-start.113 = (bf16[480,640]{1,0:T(8,128)(2,1)S(1)}, bf16[480,640]{1,0:T(8,128)(2,1)S(1)}, u32[]{:S(2)}, u32[]{:S(2)}) collective-permute-start(bf16[480,640]{1,0:T(8,128)(2,1)S(1)} %get-tuple-element.803), channel_id=1, source_target_pairs={{2,0},{3,1},{4,2},{5,3},{6,4},{7,5},{10,8},{11,9},{12,10},{13,11},... | collective-permute-start | bytes 1843208 | tf_op jit(solution)/shard_map/cond/branch_2_fun/ppermute | solution.py:391
  313.3 131.0 %collective-permute-start.114 = (bf16[480,640]{1,0:T(8,128)(2,1)S(1)}, bf16[480,640]{1,0:T(8,128)(2,1)S(1)}, u32[]{:S(2)}, u32[]{:S(2)}) collective-permute-start(bf16[480,640]{1,0:T(8,128)(2,1)S(1)} %collective-permute-done.108.refs_1_), channel_id=1, source_target_pairs={{0,1},{1,0},{2,3},{3,2},{4,5},{5,4},{6,7},{7,6},{8,9},{9,8},{10,11... | collective-permute-start | bytes 1843208 | tf_op jit(solution)/shard_map/cond/branch_2_fun/ppermute | solution.py:406
  315.0 129.3 %collective-permute-start.115 = (bf16[480,640]{1,0:T(8,128)(2,1)S(1)}, bf16[480,640]{1,0:T(8,128)(2,1)S(1)}, u32[]{:S(2)}, u32[]{:S(2)}) collective-permute-start(bf16[480,640]{1,0:T(8,128)(2,1)S(1)} %collective-permute-done.109.refs_2_), channel_id=1, source_target_pairs={{0,1},{1,0},{2,3},{3,2},{4,5},{5,4},{6,7},{7,6},{8,9},{9,8},{10,11... | collective-permute-start | bytes 1843208 | tf_op jit(solution)/shard_map/cond/branch_2_fun/ppermute | solution.py:406
  317.2 134.5 %collective-permute-start.120 = (bf16[480,640]{1,0:T(8,128)(2,1)S(1)}, bf16[480,640]{1,0:T(8,128)(2,1)S(1)}, u32[]{:S(2)}, u32[]{:S(2)}) collective-permute-start(bf16[480,640]{1,0:T(8,128)(2,1)S(1)} %get-tuple-element.807), channel_id=1, source_target_pairs={{0,2},{1,3},{2,4},{3,5},{4,6},{5,7},{8,10},{9,11},{10,12},{11,13},... | collective-permute-start | bytes 1843208 | tf_op jit(solution)/shard_map/cond/branch_2_fun/ppermute | solution.py:391
  451.6 20.2 %collective-permute-start.118 = (bf16[480,640]{1,0:T(8,128)(2,1)S(1)}, bf16[480,640]{1,0:T(8,128)(2,1)}, u32[]{:S(2)}, u32[]{:S(2)}) collective-permute-start(bf16[480,640]{1,0:T(8,128)(2,1)S(1)} %get-tuple-element.805), channel_id=1, source_target_pairs={{2,0},{3,1},{4,2},{5,3},{6,4},{7,5},{10,8},{11,9},{12,10},{13,11},... | collective-permute-start | bytes 1843208 | tf_op jit(solution)/shard_map/cond/branch_2_fun/ppermute | solution.py:391
  458.6 154.9 %collective-permute-start.126 = (bf16[1024,640]{1,0:T(8,128)(2,1)}, bf16[1024,640]{1,0:T(8,128)(2,1)S(1)}, u32[]{:S(2)}, u32[]{:S(2)}) collective-permute-start(bf16[1024,640]{1,0:T(8,128)(2,1)} %get-tuple-element.810), channel_id=1, source_target_pairs={{0,8},{8,16},{16,24},{24,0},{1,9},{9,17},{17,25},{25,1},{2,10},{10... | collective-permute-start | bytes 3932168 | tf_op jit(solution)/shard_map/cond/branch_2_fun/ppermute | solution.py:469
  459.5 154.0 %collective-permute-start.127 = (bf16[1024,640]{1,0:T(8,128)(2,1)}, bf16[1024,640]{1,0:T(8,128)(2,1)S(1)}, u32[]{:S(2)}, u32[]{:S(2)}) collective-permute-start(bf16[1024,640]{1,0:T(8,128)(2,1)} %get-tuple-element.811), channel_id=1, source_target_pairs={{0,16},{8,24},{16,0},{24,8},{1,17},{9,25},{17,1},{25,9},{2,18},{10... | collective-permute-start | bytes 3932168 | tf_op jit(solution)/shard_map/cond/branch_2_fun/ppermute | solution.py:469
  460.3 153.2 %collective-permute-start.128 = (bf16[1024,640]{1,0:T(8,128)(2,1)}, bf16[1024,640]{1,0:T(8,128)(2,1)}, u32[]{:S(2)}, u32[]{:S(2)}) collective-permute-start(bf16[1024,640]{1,0:T(8,128)(2,1)} %get-tuple-element.812), channel_id=1, source_target_pairs={{0,24},{8,0},{16,8},{24,16},{1,25},{9,1},{17,9},{25,17},{2,26},{10... | collective-permute-start | bytes 3932168 | tf_op jit(solution)/shard_map/cond/branch_2_fun/ppermute | solution.py:469
  473.8 101.4 %collective-permute-start.117 = (bf16[480,640]{1,0:T(8,128)(2,1)}, bf16[480,640]{1,0:T(8,128)(2,1)}, u32[]{:S(2)}, u32[]{:S(2)}) collective-permute-start(bf16[480,640]{1,0:T(8,128)(2,1)} %collective-permute-done.116.refs_1_), channel_id=1, source_target_pairs={{0,1},{1,0},{2,3},{3,2},{4,5},{5,4},{6,7},{7,6},{8,9},{9,8},{10,11... | collective-permute-start | bytes 1843208 | tf_op jit(solution)/shard_map/cond/branch_2_fun/ppermute | solution.py:406
  475.5 99.6 %collective-permute-start.119 = (bf16[480,640]{1,0:T(8,128)(2,1)}, bf16[480,640]{1,0:T(8,128)(2,1)}, u32[]{:S(2)}, u32[]{:S(2)}) collective-permute-start(bf16[480,640]{1,0:T(8,128)(2,1)} %collective-permute-done.118.refs_2_), channel_id=1, source_target_pairs={{0,1},{1,0},{2,3},{3,2},{4,5},{5,4},{6,7},{7,6},{8,9},{9,8},{10,11... | collective-permute-start | bytes 1843208 | tf_op jit(solution)/shard_map/cond/branch_2_fun/ppermute | solution.py:406
  (41 other events, 677.7 us)
